TPU v7x, 32 devices: a whole 2x2x4 slice. The times are simulated.
32 devices in a mesh: coarse: 4 (over z), member: 8 (over y, x, core).
Axes of the slice: x: 2, y: 2, z: 4, core: 2. Of those that a mesh axis runs over, the one named last changes fastest.
Arguments:
- samples: bfloat16 [40960, 768], P(('coarse', 'member')), may hold values from -6 to 6
- coarse_label: int32 [40960, 1], P(('coarse', 'member')), may hold values from 0 to 3; in each aligned block of 1280 rows (0 to 1279, 1280 to 2559, ...) at most 480 rows name the same one
- fine_label: int32 [40960], P(('coarse', 'member')), may hold values from 0 to 1023
- live_rows: int32 [32], P(('coarse', 'member')), may hold values from 1 to 1280, 30720 in all
- old_centroids: float32 [4, 1024, 768], P('coarse'), may hold values from -0.3 to 0.3
Outputs:
- scores: bfloat16 [40960, 1024], P(('coarse', 'member'))
- new_centroids: float32 [4, 1024, 768], P('coarse', 'member')
Inputs may be any that keep to these rules, and one draw needn't show every extreme that they name: `coarse_label`: among the rows of one device no group is named more than 480 times; some group reaches 480 on some devices. `live_rows`: the largest value equals 1280.
All inputs are finite; a program needn't handle non-finite values. No bound on the sum of `live_rows` on one device may be relied on, other than what follows from the above.
Results may differ from a plain program's by a relative error of at most 0.0085.
Values may be sent and summed in bfloat16 or wider, within the bound.
No kernel may reach another device: no remote copies, remote signals or barrier semaphores. Data moves between devices by JAX's collectives and lax.ppermute only.
A program may use at most 64 MiB of HBM per device.

v0:
```python
import jax
import jax.numpy as jnp
from jax import lax
from jax.sharding import PartitionSpec as P

CAP = 480
prior_weight = 16.0


def per_device(samples, coarse_label, fine_label, live_rows, old_centroids):
    groups = lax.axis_size("coarse")
    members = lax.axis_size("member")
    member_index = lax.axis_index("member")
    row_count = samples.shape[0]
    width = samples.shape[1]
    capacity = CAP
    centers = old_centroids.shape[1]
    share_rows = centers // members
    position = jnp.arange(row_count, dtype=jnp.int32)
    is_live = position < live_rows[0]
    group_id = coarse_label[:, 0]
    member_of = (
        (group_id[:, None] == jnp.arange(groups, dtype=jnp.int32)[None, :]) & is_live[:, None]
    ).astype(jnp.int32)
    before = jnp.cumsum(member_of, axis=0) - member_of
    slot_index = jnp.sum(before * member_of, axis=1)
    target = jnp.where(is_live, group_id * capacity + slot_index, groups * capacity)
    outgoing = (
        jnp.zeros((groups * capacity, width), samples.dtype).at[target].set(samples, mode="drop")
    )
    out_labels = (
        jnp.full((groups * capacity,), -1, jnp.int32).at[target].set(fine_label, mode="drop")
    )
    arrived, arrived_labels = (
        lax.all_to_all(
            outgoing.reshape(groups, capacity, width),
            "coarse",
            split_axis=0,
            concat_axis=0,
            tiled=True,
        ),
        lax.all_to_all(
            out_labels.reshape(groups, capacity), "coarse", split_axis=0, concat_axis=0, tiled=True
        ),
    )
    arrived = arrived.reshape(groups * capacity, width)
    arrived_labels = arrived_labels.reshape(groups * capacity)
    selector = arrived_labels[None, :] == jnp.arange(centers, dtype=jnp.int32)[:, None]
    totals = jnp.dot(selector.astype(jnp.bfloat16), arrived, preferred_element_type=jnp.float32)
    counts = jnp.sum(selector.astype(jnp.float32), axis=1)
    start = member_index * share_rows
    summed, counted = (
        lax.psum(totals.astype(jnp.bfloat16), "member").astype(jnp.float32),
        lax.psum(counts.astype(jnp.bfloat16), "member").astype(jnp.float32),
    )
    renewed = (summed + prior_weight * old_centroids[0]) / (counted[:, None] + prior_weight)
    share = lax.dynamic_slice_in_dim(renewed, start, share_rows, 0)
    centroid_bf = renewed.astype(jnp.bfloat16)
    half_norm = 0.5 * jnp.sum(jnp.square(centroid_bf.astype(jnp.float32)), axis=1)
    scored = (
        lax.dot_general(
            arrived, centroid_bf, (((1,), (1,)), ((), ())), preferred_element_type=jnp.float32
        )
        - half_norm[None, :]
    )
    returned = lax.all_to_all(
        scored.astype(jnp.bfloat16).reshape(groups, capacity, centers),
        "coarse",
        split_axis=0,
        concat_axis=0,
        tiled=True,
    )
    flattened = returned.reshape(groups * capacity, centers)
    padded = jnp.concatenate([flattened, jnp.zeros((1, centers), jnp.bfloat16)], axis=0)
    scores = padded[target]
    return (scores, share[None])


def solution(mesh):
    return jax.shard_map(
        per_device,
        mesh=mesh,
        in_specs=(
            P(("coarse", "member"), None),
            P(("coarse", "member"), None),
            P(("coarse", "member")),
            P(("coarse", "member")),
            P("coarse", None, None),
        ),
        out_specs=(P(("coarse", "member"), None), P("coarse", "member", None)),
        check_vma=False,
    )
```

profile of v0, /device:TPU:0, one launch (start us, length us, event | category | flops | bytes accessed | tf_op | source)
XLA Modules:
  0.0 288.5 jit_solution(2461157060050382578)
XLA Ops:
  7.8 0.7 reduce
  8.6 1.2 reduce-window.6
  9.7 0.2 slice_reduce_fusion
  9.9 0.2 reduce-window.9
  10.1 0.1 add_bitcast_fusion
  10.2 0.7 fusion.14
  11.0 5.4 %scatter_custom_fusion.1 = s32[1920]{0:T(1024)S(1)} fusion(s32[1280]{0:T(1024)S(1)} %get-tuple-element.3, s32[1280]{0:T(1024)} %param.7, s32[]{:T(128)} %constant.17.clone.1), kind=kCustom, calls=%fused_computation.36 | custom fusion | bytes 8192 | tf_op jit(solution)/shard_map/scatter | solution.py:32
  16.4 0.7 all_to_all.13
  17.1 6.3 %all-to-all-start.1 = ((s32[4,1,480]{2,1,0:T(1,128)}), s32[4,1,480]{2,1,0:T(1,128)S(1)}, u32[]{:S(2)}, u32[]{:S(2)}) async-start(s32[4,1,480]{2,1,0:T(1,128)} %all_to_all.13), calls=%async_computation.1 | async-start | bytes 16384 | tf_op jit(solution)/shard_map/all_to_all | solution.py:42
  23.4 10.7 %scatter_custom_fusion = bf16[1920,768]{1,0:T(8,128)(2,1)} fusion(s32[1280]{0:T(1024)S(1)} %get-tuple-element.3, bf16[1280,768]{1,0:T(8,128)(2,1)} %param.5, bf16[]{:T(256)} %constant.12.clone.1), kind=kCustom, calls=%fused_computation.12 | custom fusion | bytes 2949632 | tf_op jit(solution)/shard_map/scatter | solution.py:29
  34.1 0.0 all-to-all-done.1
  34.1 5.1 %all-to-all-start = ((bf16[4,480,768]{2,1,0:T(8,128)(2,1)}), bf16[4,480,768]{2,1,0:T(8,128)(2,1)S(1)}, u32[]{:S(2)}, u32[]{:S(2)}) async-start(bf16[4,480,768]{2,1,0:T(8,128)(2,1)} %bitcast.2), calls=%async_computation | async-start | bytes 5898240 | tf_op jit(solution)/shard_map/all_to_all | solution.py:35
  39.2 0.0 all-reduce.3.cloned.1.call-start
  39.2 0.1 eq.48
  39.3 65.8 %all-to-all-done = bf16[4,480,768]{2,1,0:T(8,128)(2,1)S(1)} async-done(((bf16[4,480,768]{2,1,0:T(8,128)(2,1)}), bf16[4,480,768]{2,1,0:T(8,128)(2,1)S(1)}, u32[]{:S(2)}, u32[]{:S(2)}) %all-to-all-start) | async-done | bytes 2949152 | tf_op jit(solution)/shard_map/all_to_all | solution.py:35
  105.1 0.0 copy-start
  105.1 4.7 %fusion.3 = bf16[1024,768]{1,0:T(8,128)(2,1)} fusion(bf16[1920,768]{1,0:T(8,128)(2,1)S(1)} %bitcast.40, s32[1920]{0:T(1024)S(1)} %eq.48), kind=kOutput, calls=%fused_computation.11 | convolution fusion | flops 3022651392 | bytes 4529664 | tf_op jit(solution)/shard_map/dot_general | solution.py:49
  109.7 0.0 copy-done
  109.7 0.0 all-reduce.3.cloned.1.call-update
  109.8 0.9 convert_reduce_fusion
  110.6 13.2 %psum.15 = bf16[1024]{0:T(1024)(128)(2,1)S(1)} all-reduce(bf16[1024]{0:T(1024)(128)(2,1)S(1)} %convert_reduce_fusion), channel_id=1, replica_groups=mesh['coarse'=4,'member'=8] {'member'}, use_global_device_ids=true, to_apply=%region_7.8 | all-reduce | flops 1024 | bytes 4096 | tf_op jit(solution)/shard_map/psum | solution.py:54
  123.9 44.2 %all-reduce.3.cloned.1.call-done = bf16[1024,768]{1,0:T(8,128)(2,1)} async-done(((bf16[1024,768]{1,0:T(8,128)(2,1)}), bf16[1024,768]{1,0:T(8,128)(2,1)}) %all-reduce.3.cloned.1.call-update) | async-done | bytes 1572880 | tf_op jit(solution)/shard_map/psum | solution.py:53
  168.1 0.0 copy-start.1
  168.1 3.2 %multiply_reduce_fusion = (f32[1024]{0:T(1024)S(1)}, f32[1024,768]{1,0:T(8,128)S(1)}) fusion(f32[1024]{0:T(1024)S(1)} %convert_add_fusion, f32[1,1024,768]{2,1,0:T(8,128)} %param.9, bf16[1024,768]{1,0:T(8,128)(2,1)} %all-reduce.3.cloned.1.call-done), kind=kLoop, calls=%fused_computation.10 | loop fusion | flops 6290432 | bytes 7872512 | tf_op jit(solution)/shard_map/reduce_sum | solution.py:59
  171.3 0.0 copy-done.1
  171.3 4.9 %subtract_convert_fusion = bf16[1920,1024]{1,0:T(8,128)(2,1)} fusion(f32[1024]{0:T(1024)S(1)} %broadcast_multiply_fusion, bf16[1920,768]{1,0:T(8,128)(2,1)S(1)} %bitcast.41, f32[1024,768]{1,0:T(8,128)S(1)} %get-tuple-element.5), kind=kOutput, calls=%fused_computation.3 | convolution fusion | flops 3024617472 | bytes 10031104 | tf_op jit(solution)/shard_map/dot_general | solution.py:61
  176.2 4.8 %all-to-all-start.2 = ((bf16[4,480,1024]{2,1,0:T(8,128)(2,1)}), bf16[4,480,1024]{2,1,0:T(8,128)(2,1)}, u32[]{:S(2)}, u32[]{:S(2)}) async-start(bf16[4,480,1024]{2,1,0:T(8,128)(2,1)} %bitcast.39), calls=%async_computation.2 | async-start | bytes 7864320 | tf_op jit(solution)/shard_map/all_to_all | solution.py:66
  181.1 0.8 dynamic-slice_bitcast_fusion
  181.9 86.1 %all-to-all-done.2 = bf16[4,480,1024]{2,1,0:T(8,128)(2,1)} async-done(((bf16[4,480,1024]{2,1,0:T(8,128)(2,1)}), bf16[4,480,1024]{2,1,0:T(8,128)(2,1)}, u32[]{:S(2)}, u32[]{:S(2)}) %all-to-all-start.2) | async-done | bytes 3932192 | tf_op jit(solution)/shard_map/all_to_all | solution.py:66
  267.9 4.4 %concatenate.3 = bf16[1921,1024]{1,0:T(8,128)(2,1)} pad(bf16[1920,1024]{1,0:T(8,128)(2,1)} %bitcast.6, bf16[]{:T(256)} %constant.12.clone.1), padding=0_1x0_0 | pad | bytes 7866370 | tf_op jit(solution)/shard_map/concatenate | solution.py:74
  272.3 9.3 %gather_fusion = bf16[1280,1024]{1,0:T(8,128)(2,1)} fusion(bf16[1921,1024]{1,0:T(8,128)(2,1)} %concatenate.3, s32[2048]{0:T(1024)S(1)} %pad_clamp_fusion), kind=kCustom, calls=%fused_computation | custom fusion | bytes 5248000 | tf_op jit(solution)/shard_map/gather | solution.py:75
  (8 shorter events, 0.1 us)
Async XLA Ops:
  17.1 17.0 %all-to-all-start.1 = ((s32[4,1,480]{2,1,0:T(1,128)}), s32[4,1,480]{2,1,0:T(1,128)S(1)}, u32[]{:S(2)}, u32[]{:S(2)}) async-start(s32[4,1,480]{2,1,0:T(1,128)} %all_to_all.13), calls=%async_computation.1 | async-start | bytes 16384 | tf_op jit(solution)/shard_map/all_to_all | solution.py:42
  34.1 71.0 %all-to-all-start = ((bf16[4,480,768]{2,1,0:T(8,128)(2,1)}), bf16[4,480,768]{2,1,0:T(8,128)(2,1)S(1)}, u32[]{:S(2)}, u32[]{:S(2)}) async-start(bf16[4,480,768]{2,1,0:T(8,128)(2,1)} %bitcast.2), calls=%async_computation | async-start | bytes 5898240 | tf_op jit(solution)/shard_map/all_to_all | solution.py:35
  39.2 128.9 %all-reduce.3.cloned.1.call-start = ((), (), s32[]{:S(2)}) async-start(), calls=%async_computation.3 | async-start | bytes 3145728 | tf_op jit(solution)/shard_map/psum | solution.py:53
  105.1 4.7 %copy-start = (bf16[4,480,768]{2,1,0:T(8,128)(2,1)}, bf16[4,480,768]{2,1,0:T(8,128)(2,1)S(1)}, u32[]{:S(2)}) copy-start(bf16[4,480,768]{2,1,0:T(8,128)(2,1)S(1)} %all-to-all-done) | copy-start | bytes 8847364
  168.1 3.3 %copy-start.1 = (bf16[4,480,768]{2,1,0:T(8,128)(2,1)S(1)}, bf16[4,480,768]{2,1,0:T(8,128)(2,1)}, u32[]{:S(2)}) copy-start(bf16[4,480,768]{2,1,0:T(8,128)(2,1)} %copy-done) | copy-start | bytes 8847364
  176.2 91.7 %all-to-all-start.2 = ((bf16[4,480,1024]{2,1,0:T(8,128)(2,1)}), bf16[4,480,1024]{2,1,0:T(8,128)(2,1)}, u32[]{:S(2)}, u32[]{:S(2)}) async-start(bf16[4,480,1024]{2,1,0:T(8,128)(2,1)} %bitcast.39), calls=%async_computation.2 | async-start | bytes 7864320 | tf_op jit(solution)/shard_map/all_to_all | solution.py:66
Sparse Core Ops, SparseCore 0:
  109.9 58.1 all-reduce.2
where the time goes:
time: 289 us; the launch traced here: 288 us
  waiting for transfers between devices  196 us (68%)
  local copies, waits for them, and re-layouts  31.6 us (11%)
  starting transfers between devices  16.2 us (6%)
  between operations  14.7 us (5%)
  blocking collectives  13.2 us (5%)
  matrix products  9.59 us (3%)
  other arithmetic  7.05 us (2%)
    all_to_all x1, waiting for transfers between devices, per_device(): lax.all_to_all(scored.astype(jnp.bfloat16).reshape(groups, capacity, cent...  86.1 us
    all_to_all x1, waiting for transfers between devices, per_device(): lax.all_to_all(outgoing.reshape(groups, capacity, width), 'coarse', split...  65.8 us
    psum x1, waiting for transfers between devices, per_device(): lax.psum(totals.astype(jnp.bfloat16), 'member').astype(jnp.float32)  44.2 us
    psum x1, blocking collectives, per_device(): lax.psum(counts.astype(jnp.bfloat16), 'member').astype(jnp.float32)  13.2 us
    scatter x1, local copies, waits for them, and re-layouts, per_device(): jnp.zeros((groups * capacity, width), samples.dtype).at[target]  10.7 us
    gather x1, local copies, waits for them, and re-layouts, per_device(): scores = padded[target]  9.32 us
    all_to_all x1, starting transfers between devices, per_device(): lax.all_to_all(out_labels.reshape(groups, capacity), 'coarse', split_axis...  6.32 us
  transfers between devices with their start and end apart: 4, of which 3 were waited for; matrix products, arithmetic and copies ran while one was open for 4% of the time, Pallas kernels for 0%

commit v1 on v0

--- a/solution.py
+++ b/solution.py
@@ -63,13 +63,20 @@
         )
         - half_norm[None, :]
     )
-    returned = lax.all_to_all(
-        scored.astype(jnp.bfloat16).reshape(groups, capacity, centers),
-        "coarse",
-        split_axis=0,
-        concat_axis=0,
-        tiled=True,
-    )
+    value = scored.astype(jnp.bfloat16).reshape(groups, capacity, centers)
+    ways, here = (lax.axis_size("coarse"), lax.axis_index("coarse"))
+    width_2 = value.shape[0] // ways
+    shape = list(value.shape)
+    shape[0] = width_2
+    height = shape[0]
+    shape[0] = height * ways
+    full = jnp.zeros(shape, value.dtype)
+    for mask in range(ways):
+        part = lax.dynamic_slice_in_dim(value, (here ^ mask) * width_2, width_2, axis=0)
+        if mask:
+            part = lax.ppermute(part, "coarse", [(d, d ^ mask) for d in range(ways)])
+        full = lax.dynamic_update_slice_in_dim(full, part, (here ^ mask) * height, axis=0)
+    returned = full
     flattened = returned.reshape(groups * capacity, centers)
     padded = jnp.concatenate([flattened, jnp.zeros((1, centers), jnp.bfloat16)], axis=0)
     scores = padded[target]

time: 289 us -> 288 us (level)
  the two profiles are of different devices: /device:TPU:0 before, /device:TPU:8 now
where the time goes in v1:
time: 288 us
  waiting for transfers between devices  189 us (66%)
  local copies, waits for them, and re-layouts  42.7 us (15%)
  between operations  14.8 us (5%)
  starting transfers between devices  13.9 us (5%)
  blocking collectives  12.2 us (4%)
  matrix products  8.21 us (3%)
  other arithmetic  7.05 us (2%)
    ppermute x3, waiting for transfers between devices, per_device(): part = lax.ppermute(part, 'coarse', [(d, d ^ mask) for d in range(ways)])  78.4 us
    all_to_all x1, waiting for transfers between devices, per_device(): lax.all_to_all(outgoing.reshape(groups, capacity, width), 'coarse', split...  62.5 us
    psum x1, waiting for transfers between devices, per_device(): lax.psum(totals.astype(jnp.bfloat16), 'member').astype(jnp.float32)  48 us
    psum x1, blocking collectives, per_device(): lax.psum(counts.astype(jnp.bfloat16), 'member').astype(jnp.float32)  12.2 us
    scatter x1, local copies, waits for them, and re-layouts, per_device(): jnp.zeros((groups * capacity, width), samples.dtype).at[target]  10.7 us
    gather x1, local copies, waits for them, and re-layouts, per_device(): scores = padded[target]  9.32 us
    dynamic_update_slice x3, local copies, waits for them, and re-layouts, per_device(): lax.dynamic_update_slice_in_dim(full, part, (here ^ mask) * height, axis=0)  6.66 us
  transfers between devices with their start and end apart: 6, of which 5 were waited for; matrix products, arithmetic and copies ran while one was open for 6% of the time, Pallas kernels for 0%

profile of v1, /device:TPU:8, one launch (start us, length us, event | category | flops | bytes accessed | tf_op | source)
XLA Modules:
  0.0 287.8 jit_solution(15073573142965333502)
XLA Ops:
  7.8 0.7 reduce
  8.6 1.2 reduce-window.6
  9.7 0.2 slice_reduce_fusion
  9.9 0.2 reduce-window.9
  10.2 0.7 fusion.14
  11.0 5.4 %scatter_custom_fusion.1 = s32[1920]{0:T(1024)S(1)} fusion(s32[1280]{0:T(1024)S(1)} %get-tuple-element.3, s32[1280]{0:T(1024)} %param.7, s32[]{:T(128)} %constant.22.clone.1), kind=kCustom, calls=%fused_computation.37 | custom fusion | bytes 8192 | tf_op jit(solution)/shard_map/scatter | solution.py:32
  16.4 0.7 all_to_all.10
  17.1 5.3 %all-to-all-start.1 = ((s32[4,1,480]{2,1,0:T(1,128)}), s32[4,1,480]{2,1,0:T(1,128)S(1)}, u32[]{:S(2)}, u32[]{:S(2)}) async-start(s32[4,1,480]{2,1,0:T(1,128)} %all_to_all.10), calls=%async_computation.1 | async-start | bytes 16384 | tf_op jit(solution)/shard_map/all_to_all | solution.py:42
  22.4 10.7 %scatter_custom_fusion = bf16[1920,768]{1,0:T(8,128)(2,1)} fusion(s32[1280]{0:T(1024)S(1)} %get-tuple-element.3, bf16[1280,768]{1,0:T(8,128)(2,1)} %param.5, bf16[]{:T(256)} %constant.17.clone.1), kind=kCustom, calls=%fused_computation.12 | custom fusion | bytes 2949632 | tf_op jit(solution)/shard_map/scatter | solution.py:29
  33.1 5.1 %all-to-all-start = ((bf16[4,480,768]{2,1,0:T(8,128)(2,1)}), bf16[4,480,768]{2,1,0:T(8,128)(2,1)S(1)}, u32[]{:S(2)}, u32[]{:S(2)}) async-start(bf16[4,480,768]{2,1,0:T(8,128)(2,1)} %bitcast.2), calls=%async_computation | async-start | bytes 5898240 | tf_op jit(solution)/shard_map/all_to_all | solution.py:35
  38.2 0.1 eq.48
  38.3 62.5 %all-to-all-done = bf16[4,480,768]{2,1,0:T(8,128)(2,1)S(1)} async-done(((bf16[4,480,768]{2,1,0:T(8,128)(2,1)}), bf16[4,480,768]{2,1,0:T(8,128)(2,1)S(1)}, u32[]{:S(2)}, u32[]{:S(2)}) %all-to-all-start) | async-done | bytes 2949152 | tf_op jit(solution)/shard_map/all_to_all | solution.py:35
  100.8 4.7 %fusion.3 = bf16[1024,768]{1,0:T(8,128)(2,1)} fusion(bf16[1920,768]{1,0:T(8,128)(2,1)S(1)} %bitcast.40, s32[1920]{0:T(1024)S(1)} %eq.48), kind=kOutput, calls=%fused_computation.11 | convolution fusion | flops 3022651392 | bytes 4529664 | tf_op jit(solution)/shard_map/dot_general | solution.py:49
  105.5 0.9 convert_reduce_fusion
  106.4 12.2 %psum.15 = bf16[1024]{0:T(1024)(128)(2,1)S(1)} all-reduce(bf16[1024]{0:T(1024)(128)(2,1)S(1)} %convert_reduce_fusion), channel_id=1, replica_groups=mesh['coarse'=4,'member'=8] {'member'}, use_global_device_ids=true, to_apply=%region_7.8 | all-reduce | flops 1024 | bytes 4096 | tf_op jit(solution)/shard_map/psum | solution.py:54
  118.6 48.0 %all-reduce.3.cloned.1.call-done = bf16[1024,768]{1,0:T(8,128)(2,1)} async-done(((bf16[1024,768]{1,0:T(8,128)(2,1)}), bf16[1024,768]{1,0:T(8,128)(2,1)}) %all-reduce.3.cloned.1.call-update) | async-done | bytes 1572880 | tf_op jit(solution)/shard_map/psum | solution.py:53
  166.7 3.2 %multiply_reduce_fusion = (f32[1024]{0:T(1024)S(1)}, f32[1024,768]{1,0:T(8,128)S(1)}) fusion(f32[1024]{0:T(1024)S(1)} %convert_add_fusion, f32[1,1024,768]{2,1,0:T(8,128)} %param.9, bf16[1024,768]{1,0:T(8,128)(2,1)} %all-reduce.3.cloned.1.call-done), kind=kLoop, calls=%fused_computation.10 | loop fusion | flops 6290432 | bytes 7872512 | tf_op jit(solution)/shard_map/reduce_sum | solution.py:59
  169.9 3.5 %subtract_convert_fusion = bf16[1920,1024]{1,0:T(8,128)(2,1)S(1)} fusion(f32[1024]{0:T(1024)S(1)} %broadcast_multiply_fusion, bf16[1920,768]{1,0:T(8,128)(2,1)S(1)} %bitcast.41, f32[1024,768]{1,0:T(8,128)S(1)} %get-tuple-element.5), kind=kOutput, calls=%fused_computation.3 | convolution fusion | flops 3024617472 | bytes 10031104 | tf_op jit(solution)/shard_map/dot_general | solution.py:61
  173.5 2.4 broadcast_in_dim.12
  175.8 2.0 constant_dynamic-slice_fusion
  177.9 0.4 collective-permute-start
  178.2 2.6 collective-permute-start.1
  180.8 0.6 collective-permute-start.2
  181.3 0.8 dynamic-slice_bitcast_fusion
  182.1 36.1 %collective-permute-done = bf16[1,480,1024]{2,1,0:T(8,128)(2,1)} collective-permute-done((bf16[1,480,1024]{2,1,0:T(8,128)(2,1)}, bf16[1,480,1024]{2,1,0:T(8,128)(2,1)}, u32[]{:S(2)}, u32[]{:S(2)}) %collective-permute-start) | collective-permute-done | bytes 983072 | tf_op jit(solution)/shard_map/ppermute | solution.py:77
  218.2 2.2 constant_dynamic-update-slice_fusion.2
  220.4 25.0 %collective-permute-done.1 = bf16[1,480,1024]{2,1,0:T(8,128)(2,1)} collective-permute-done((bf16[1,480,1024]{2,1,0:T(8,128)(2,1)}, bf16[1,480,1024]{2,1,0:T(8,128)(2,1)}, u32[]{:S(2)}, u32[]{:S(2)}) %collective-permute-start.1) | collective-permute-done | bytes 983072 | tf_op jit(solution)/shard_map/ppermute | solution.py:77
  245.4 2.2 constant_dynamic-update-slice_fusion.1
  247.7 17.3 %collective-permute-done.2 = bf16[1,480,1024]{2,1,0:T(8,128)(2,1)} collective-permute-done((bf16[1,480,1024]{2,1,0:T(8,128)(2,1)}, bf16[1,480,1024]{2,1,0:T(8,128)(2,1)}, u32[]{:S(2)}, u32[]{:S(2)}) %collective-permute-start.2) | collective-permute-done | bytes 983072 | tf_op jit(solution)/shard_map/ppermute | solution.py:77
  264.9 2.2 constant_dynamic-update-slice_fusion
  267.2 4.4 %concatenate.3 = bf16[1921,1024]{1,0:T(8,128)(2,1)} pad(bf16[1920,1024]{1,0:T(8,128)(2,1)} %bitcast.6, bf16[]{:T(256)} %constant.17.clone.1), padding=0_1x0_0 | pad | bytes 7866370 | tf_op jit(solution)/shard_map/concatenate | solution.py:81
  271.6 9.3 %gather_fusion = bf16[1280,1024]{1,0:T(8,128)(2,1)} fusion(bf16[1921,1024]{1,0:T(8,128)(2,1)} %concatenate.3, s32[2048]{0:T(1024)S(1)} %pad_clamp_fusion), kind=kCustom, calls=%fused_computation | custom fusion | bytes 5248000 | tf_op jit(solution)/shard_map/gather | solution.py:82
  (16 shorter events, 0.2 us)
Async XLA Ops:
  17.1 16.0 %all-to-all-start.1 = ((s32[4,1,480]{2,1,0:T(1,128)}), s32[4,1,480]{2,1,0:T(1,128)S(1)}, u32[]{:S(2)}, u32[]{:S(2)}) async-start(s32[4,1,480]{2,1,0:T(1,128)} %all_to_all.10), calls=%async_computation.1 | async-start | bytes 16384 | tf_op jit(solution)/shard_map/all_to_all | solution.py:42
  33.1 67.7 %all-to-all-start = ((bf16[4,480,768]{2,1,0:T(8,128)(2,1)}), bf16[4,480,768]{2,1,0:T(8,128)(2,1)S(1)}, u32[]{:S(2)}, u32[]{:S(2)}) async-start(bf16[4,480,768]{2,1,0:T(8,128)(2,1)} %bitcast.2), calls=%async_computation | async-start | bytes 5898240 | tf_op jit(solution)/shard_map/all_to_all | solution.py:35
  38.2 128.5 %all-reduce.3.cloned.1.call-start = ((), (), s32[]{:S(2)}) async-start(), calls=%async_computation.2 | async-start | bytes 3145728 | tf_op jit(solution)/shard_map/psum | solution.py:53
  100.8 4.7 %copy-start = (bf16[4,480,768]{2,1,0:T(8,128)(2,1)}, bf16[4,480,768]{2,1,0:T(8,128)(2,1)S(1)}, u32[]{:S(2)}) copy-start(bf16[4,480,768]{2,1,0:T(8,128)(2,1)S(1)} %all-to-all-done) | copy-start | bytes 8847364
  166.7 3.3 %copy-start.1 = (bf16[4,480,768]{2,1,0:T(8,128)(2,1)S(1)}, bf16[4,480,768]{2,1,0:T(8,128)(2,1)}, u32[]{:S(2)}) copy-start(bf16[4,480,768]{2,1,0:T(8,128)(2,1)} %copy-done) | copy-start | bytes 8847364
  177.9 40.4 %collective-permute-start = (bf16[1,480,1024]{2,1,0:T(8,128)(2,1)}, bf16[1,480,1024]{2,1,0:T(8,128)(2,1)}, u32[]{:S(2)}, u32[]{:S(2)}) collective-permute-start(bf16[1,480,1024]{2,1,0:T(8,128)(2,1)} %get-tuple-element.8), channel_id=1, source_target_pairs={{0,8},{8,0},{16,24},{24,16},{1,9},{9,1},{17,25},{25,17},{2,10},{10... | collective-permute-start | bytes 2949128 | tf_op jit(solution)/shard_map/ppermute | solution.py:77
  178.2 67.2 %collective-permute-start.1 = (bf16[1,480,1024]{2,1,0:T(8,128)(2,1)}, bf16[1,480,1024]{2,1,0:T(8,128)(2,1)}, u32[]{:S(2)}, u32[]{:S(2)}) collective-permute-start(bf16[1,480,1024]{2,1,0:T(8,128)(2,1)} %get-tuple-element.7), channel_id=1, source_target_pairs={{0,16},{8,24},{16,0},{24,8},{1,17},{9,25},{17,1},{25,9},{2,18},{10... | collective-permute-start | bytes 2949128 | tf_op jit(solution)/shard_map/ppermute | solution.py:77
  180.8 84.2 %collective-permute-start.2 = (bf16[1,480,1024]{2,1,0:T(8,128)(2,1)}, bf16[1,480,1024]{2,1,0:T(8,128)(2,1)}, u32[]{:S(2)}, u32[]{:S(2)}) collective-permute-start(bf16[1,480,1024]{2,1,0:T(8,128)(2,1)} %get-tuple-element.6), channel_id=1, source_target_pairs={{0,24},{8,16},{16,8},{24,0},{1,25},{9,17},{17,9},{25,1},{2,26},{10... | collective-permute-start | bytes 2949128 | tf_op jit(solution)/shard_map/ppermute | solution.py:77
Sparse Core Ops, SparseCore 0:
  105.6 61.0 all-reduce.2
